TPU v7x, 32 devices: a whole 2x2x4 slice. The times are simulated.
32 devices in a mesh: groups: 2 (over x), adapt: 16 (over z, y, core).
Axes of the slice: x: 2, y: 2, z: 4, core: 2. Of those that a mesh axis runs over, the one named last changes fastest.
Arguments:
- tokens: bfloat16 [16384, 5120], P(('groups', 'adapt')), parts along dimension 0, may hold values from -6 to 6
- lengths: int32 [32, 8], P(('groups', 'adapt')), parts along dimension 0, may hold values from 1 to 256, 512 in all within a row
- active: int32 [32, 4], P(('groups', 'adapt')), parts along dimension 0, may hold values from 0 to 31
- program_adapter_slot: int32 [32, 8], P(('groups', 'adapt')), parts along dimension 0, may hold values from 0 to 3
- base_weight: bfloat16 [5120, 512], replicated, may hold values from -0.078125 to 0.078125
- adapter_down: bfloat16 [64, 327680], P('groups', 'adapt'), parts along dimension 0, may hold values from -0.078125 to 0.078125
- adapter_up: bfloat16 [64, 32768], P('groups', 'adapt'), parts along dimension 0, may hold values from -0.75 to 0.75
Outputs:
- values: bfloat16 [16384, 512], P(('groups', 'adapt')), parts along dimension 0
There are 2 independent parts, one for each index of `groups`. A program takes and returns all parts, laid end to end along the dimension named above; an argument that names none is the same for every part. Nothing has to cross between parts.
Inputs may be any that keep to these rules, and one draw needn't show every extreme that they name: Each device's lengths sum to 512; the longest program of each device has 256 rows. `active`: ids of stored adapters; some are common.
All inputs are finite; a program needn't handle non-finite values.
Results may differ from a plain program's by a relative error of at most 0.0075.
Values may be sent and summed in bfloat16 or wider, within the bound.
A program may use at most 128 MiB of HBM per device.

v0:
```python
import math

import jax
import jax.numpy as jnp
from jax import lax
from jax.sharding import PartitionSpec as P

D = 5120
KV = 512
R = 64
ACTIVE = 4


adapter_scale = 2.0


def row_slots(program_lengths, program_slots, row_count):
    programs = program_lengths.shape[0]
    program_ends = jnp.cumsum(program_lengths)
    position = lax.broadcasted_iota(jnp.int32, (row_count, programs), 0)
    program = jnp.sum((position >= program_ends[None, :]).astype(jnp.int32), axis=1)
    owner_mask = (
        program[:, None] == lax.broadcasted_iota(jnp.int32, (row_count, programs), 1)
    ).astype(jnp.int32)
    return jnp.sum(owner_mask * program_slots[None, :], axis=1)


def slot_onehot(program_lengths, program_slots, row_count, slot_count):
    row_slot = row_slots(program_lengths, program_slots, row_count)
    return (
        row_slot[:, None] == lax.broadcasted_iota(jnp.int32, (row_count, slot_count), 1)
    ).astype(jnp.float32)


def shards(tokens, lengths, active, program_adapter_slot, base_weight, adapter_down, adapter_up):
    row_count = tokens.shape[0]
    devices = lax.axis_size("adapt")
    d_local = D // devices
    row_slot = row_slots(lengths[0], program_adapter_slot[0], row_count)
    slot_hits = (
        row_slot[:, None] == lax.broadcasted_iota(jnp.int32, (row_count, ACTIVE), 1)
    ).astype(jnp.int32)
    slot_counts = jnp.sum(slot_hits, axis=0)
    order = jnp.argsort(row_slot, stable=True)
    inverse = jnp.argsort(order)
    active_lists = lax.all_gather(active, "adapt", axis=0, tiled=True)
    flat_ids = active_lists.reshape(-1)
    layouts = (
        lax.all_gather(lengths, "adapt", axis=0, tiled=True),
        lax.all_gather(program_adapter_slot, "adapt", axis=0, tiled=True),
    )
    moved = lax.all_to_all(tokens, "adapt", split_axis=1, concat_axis=0, tiled=True)
    down_local = adapter_down.reshape(adapter_down.shape[0], d_local, R)
    block_devices = lax.axis_size("adapt") * row_count // row_count
    group_size = math.gcd(block_devices, 8)

    def single_slot_selector(group_lengths, group_slots):
        return slot_onehot(group_lengths, group_slots, row_count, ACTIVE)

    def one_group(slot_group_index):
        begin = slot_group_index * group_size
        features = lax.dynamic_slice_in_dim(moved, begin * row_count, group_size * row_count, 0)
        features = features.reshape(group_size, row_count, d_local)
        group_ids = lax.dynamic_slice_in_dim(active_lists, begin, group_size, 0)
        group_lengths = lax.dynamic_slice_in_dim(layouts[0], begin, group_size, 0)
        group_slots = lax.dynamic_slice_in_dim(layouts[1], begin, group_size, 0)
        factors = down_local[group_ids]
        wide = jnp.einsum("gtd,gjdr->gtjr", features, factors, preferred_element_type=jnp.float32)
        picks = jax.vmap(single_slot_selector)(group_lengths, group_slots)
        return jnp.sum(picks[:, :, :, None] * wide, axis=2).reshape(group_size * row_count, R)

    pieces = lax.map(one_group, jnp.arange(block_devices // group_size, dtype=jnp.int32))
    low_rank = lax.psum_scatter(
        pieces.reshape(lax.axis_size("adapt") * row_count, R),
        "adapt",
        scatter_dimension=0,
        tiled=True,
    ).astype(jnp.bfloat16)
    low_sorted = low_rank[order]
    up_recv = lax.all_to_all(adapter_up[flat_ids], "adapt", split_axis=0, concat_axis=1, tiled=True)
    up_mats = jnp.transpose(up_recv.reshape(ACTIVE, KV, R), (0, 2, 1))
    delta_sorted = lax.ragged_dot(
        low_sorted, up_mats, slot_counts, preferred_element_type=jnp.float32
    )
    adapter_update = delta_sorted[inverse]
    frozen_output = jnp.dot(tokens, base_weight, preferred_element_type=jnp.float32)
    return (frozen_output + adapter_scale * adapter_update).astype(jnp.bfloat16)


def solution(mesh):
    in_specs = (
        P(("groups", "adapt"), None),
        P(("groups", "adapt"), None),
        P(("groups", "adapt"), None),
        P(("groups", "adapt"), None),
        P(),
        P("groups", "adapt"),
        P("groups", "adapt"),
    )
    out_specs = P(("groups", "adapt"), None)
    return jax.shard_map(shards, mesh=mesh, in_specs=in_specs, out_specs=out_specs, check_vma=False)
```

profile of v0, /device:TPU:0, one launch (start us, length us, event | category | flops | bytes accessed | tf_op | source)
XLA Modules:
  0.0 327.4 jit_solution(1326221487124317447)
XLA Ops:
  6.5 8.0 %copy.70 = bf16[512,5120]{0,1:T(8,128)(2,1)} copy(bf16[512,5120]{1,0:T(8,128)(2,1)} %param.9) | data formatting | bytes 10485760 | tf_op args[0]
  14.5 7.6 %all-to-all-start = ((bf16[512,16,320]{0,2,1:T(8,128)(2,1)}), bf16[512,16,320]{0,2,1:T(8,128)(2,1)}, u32[]{:S(2)}, u32[]{:S(2)}) async-start(bf16[512,16,320]{0,2,1:T(8,128)(2,1)} %bitcast.55), calls=%async_computation | async-start | bytes 10485760 | tf_op jit(solution)/shard_map/all_to_all | solution.py:52
  22.1 0.0 copy-start.5
  22.1 0.0 copy-start.3
  22.1 0.0 reduce-scatter.2.cloned.1.call-start
  22.2 3.9 %reshape.96 = bf16[32,320,64]{2,1,0:T(8,128)(2,1)} reshape(bf16[32,20480]{1,0:T(8,128)(2,1)S(1)} %copy-done.2) | data formatting | bytes 2621440 | tf_op jit(solution)/shard_map/reshape | solution.py:53
  26.1 96.7 %all-gather.2 = s32[16,1,4]{2,1,0:T(1,128)S(1)} all-gather(s32[1,1,4]{2,1,0:T(1,128)S(1)} %bitcast.65), channel_id=1, replica_groups=mesh['groups'=2,'adapt'=16] {'adapt'}, dimensions={0}, use_global_device_ids=true | all-gather | bytes 272 | tf_op jit(solution)/shard_map/all_gather | solution.py:46
  122.8 44.0 %all-gather = s32[16,1,8]{2,1,0:T(1,128)S(1)} all-gather(s32[1,1,8]{2,1,0:T(1,128)S(1)} %bitcast.66), channel_id=1, replica_groups=mesh['groups'=2,'adapt'=16] {'adapt'}, dimensions={0}, use_global_device_ids=true | all-gather | bytes 544 | tf_op jit(solution)/shard_map/all_gather | solution.py:49
  166.8 17.3 %all-gather.1 = s32[16,1,8]{2,1,0:T(1,128)S(1)} all-gather(s32[1,1,8]{2,1,0:T(1,128)S(1)} %bitcast.63), channel_id=1, replica_groups=mesh['groups'=2,'adapt'=16] {'adapt'}, dimensions={0}, use_global_device_ids=true | all-gather | bytes 544 | tf_op jit(solution)/shard_map/all_gather | solution.py:50
  184.1 5.5 %copy.83 = bf16[16,40,8,512]{3,2,0,1:T(8,128)(2,1)} copy(bf16[16,40,8,512]{3,2,1,0:T(8,128)(2,1)} %bitcast.25) | data formatting | bytes 10485760 | tf_op jit(solution)/shard_map/all_to_all | solution.py:52
  189.6 37.0 %while.12 = (s32[]{:T(128)}, f32[2,4096,64]{1,2,0:T(8,128)}, s32[2]{0:T(128)S(1)}, s32[16,8]{1,0:T(8,128)S(1)}, s32[16,8]{1,0:T(8,128)S(1)}, /*index=5*/bf16[819...) while((s32[]{:T(128)}, f32[2,4096,64]{1,2,0:T(8,128)}, ...), condition=%wide.region_5.6_spmd, body=%wide.region_0.5_spmd.sunk | while | flops 673146432 | bytes 35593252 | solution.py:72
  189.6 0.7 dynamic_slice.42
  191.0 0.1 reshape.161
  191.1 2.8 gather_fusion
  193.9 2.8 copy.92
  197.4 2.1 constant_dynamic-slice_fusion.5
  199.6 0.0 copy-done.1
  199.6 3.3 fusion.15
  202.9 0.2 reduce_window_sum.19
  203.0 0.1 convert_reduce_fusion.4
  203.1 0.1 select_reduce_fusion.3
  203.3 2.9 multiply_reduce_fusion.2
  206.2 0.6 copy.93
  206.8 0.2 broadcast_in_dim.38
  207.0 1.1 constant_dynamic-update-slice_fusion.2
  208.1 0.7 dynamic_slice.42
  209.5 0.1 reshape.161
  209.6 2.8 gather_fusion
  212.4 2.8 copy.92
  215.9 2.1 constant_dynamic-slice_fusion.5
  218.1 0.0 copy-done.1
  218.1 3.3 fusion.15
  221.4 0.2 reduce_window_sum.19
  221.5 0.1 convert_reduce_fusion.4
  221.6 0.1 select_reduce_fusion.3
  221.8 2.9 multiply_reduce_fusion.2
  224.7 0.6 copy.93
  225.3 0.2 broadcast_in_dim.38
  225.5 1.1 constant_dynamic-update-slice_fusion.2
  226.6 3.8 %copy.76 = f32[2,4096,64]{2,1,0:T(8,128)} copy(f32[2,4096,64]{1,2,0:T(8,128)} %get-tuple-element.108) | data formatting | bytes 4194304 | tf_op jit(solution)/shard_map/while | solution.py:72
  230.3 0.0 reduce-scatter.2.cloned.1.call-update
  230.4 0.5 broadcast.84
  230.9 0.7 reduce.3
  231.6 0.1 reshape.100
  231.7 0.7 gather_fusion.2
  232.4 0.8 all_to_all.30
  233.2 3.5 %all-to-all-start.1 = ((bf16[16,4,2048]{2,1,0:T(4,128)(2,1)}), bf16[16,4,2048]{2,1,0:T(4,128)(2,1)S(1)}, u32[]{:S(2)}, u32[]{:S(2)}) async-start(bf16[16,4,2048]{2,1,0:T(4,128)(2,1)} %all_to_all.30), calls=%async_computation.2 | async-start | bytes 524288 | tf_op jit(solution)/shard_map/all_to_all | solution.py:80
  236.8 0.2 reduce-window.8
  237.0 0.1 convert_reduce_fusion.1
  237.0 0.1 select_reduce_fusion.1
  237.1 3.8 %sort.34 = (s32[512]{0:T(512)}, s32[512]{0:T(512)S(1)}) sort(s32[512]{0:T(512)S(1)} %select_reduce_fusion.1, s32[512]{0:T(512)S(1)} %iota.57), dimensions={0}, to_apply=%region_10.11 | sort | flops 4608 | bytes 8192 | tf_op jit(solution)/shard_map/jit(argsort)/sort | solution.py:44
  240.9 0.6 convert_reduce_fusion.2
  241.6 1.4 ragged-dot-metadata
  242.9 3.8 %sort.35 = (s32[512]{0:T(512)}, s32[512]{0:T(512)S(1)}) sort(s32[512]{0:T(512)S(1)} %get-tuple-element.109, s32[512]{0:T(512)S(1)} %iota.59), dimensions={0}, to_apply=%region_12.13 | sort | flops 4608 | bytes 8192 | tf_op jit(solution)/shard_map/jit(argsort)/sort | solution.py:45
  246.7 0.1 all-to-all-done.1
  246.8 0.1 copy.77
  246.9 0.5 reshape.101
  247.5 0.9 copy.78
  248.4 53.2 %reduce-scatter.2.cloned.1.call-done = f32[512,64]{1,0:T(8,128)} async-done(((f32[8192,64]{1,0:T(8,128)}), f32[512,64]{1,0:T(8,128)}) %reduce-scatter.2.cloned.1.call-update) | async-done | bytes 131088 | tf_op jit(solution)/shard_map/reduce_scatter | solution.py:73
  301.6 1.0 convert_element_type.30
  302.6 1.9 gather_fusion.1
  304.5 5.2 %ragged-dot-none = f32[512,512]{1,0:T(8,128)} custom-call(s32[1]{0:T(128)} %get-tuple-element.111, s32[5]{0:T(128)} %get-tuple-element.112, s32[5]{0:T(128)} %get-tuple-element.113, s32[5]{0:T(128)} %get-tuple-element.114, s32[1]{0:T(128)} %get-tuple-element.111, bf16[512,64]{1,0:T(8,128)(2,1)} %gather_fusion.1, bf16[4,64,512]{2,1,0:T(8,128)(2,1)} %bitcast.58), custom_call_target="tpu_custom_call" | custom-call | flops 33554432 | bytes 1376272 | tf_op jit(solution)/shard_map/ragged_dot_general/ragged-dot-none
  309.6 3.2 gather_fusion.3
  312.9 7.7 %fusion.4 = bf16[512,512]{1,0:T(8,128)(2,1)} fusion(bf16[512,5120]{1,0:T(8,128)(2,1)} %param.9, bf16[5120,512]{1,0:T(8,128)(2,1)} %param.13, f32[512,512]{1,0:T(8,128)S(1)} %gather_fusion.3), kind=kOutput, calls=%fused_computation.21 | convolution fusion | flops 2685140992 | bytes 12058624 | tf_op jit(solution)/shard_map/dot_general | solution.py:86
  (29 shorter events, 0.1 us)
Async XLA Ops:
  6.5 225.1 %copy-start = (bf16[32,2048]{1,0:T(8,128)(2,1)S(1)}, bf16[32,2048]{1,0:T(8,128)(2,1)}, u32[]{:S(2)}) copy-start(bf16[32,2048]{1,0:T(8,128)(2,1)} %param.15) | copy-start | bytes 393220
  14.5 7.7 %copy-start.2 = (bf16[32,20480]{1,0:T(8,128)(2,1)S(1)}, bf16[32,20480]{1,0:T(8,128)(2,1)}, u32[]{:S(2)}) copy-start(bf16[32,20480]{1,0:T(8,128)(2,1)} %param.14) | copy-start | bytes 3932164
  14.5 169.5 %all-to-all-start = ((bf16[512,16,320]{0,2,1:T(8,128)(2,1)}), bf16[512,16,320]{0,2,1:T(8,128)(2,1)}, u32[]{:S(2)}, u32[]{:S(2)}) async-start(bf16[512,16,320]{0,2,1:T(8,128)(2,1)} %bitcast.55), calls=%async_computation | async-start | bytes 10485760 | tf_op jit(solution)/shard_map/all_to_all | solution.py:52
  22.1 4.0 %copy-start.4 = (s32[1,4]{1,0:T(1,128)S(1)}, s32[1,4]{1,0:T(1,128)}, u32[]{:S(2)}) copy-start(s32[1,4]{1,0:T(1,128)} %param.11) | copy-start | bytes 52
  22.1 100.7 %copy-start.5 = (s32[1,8]{1,0:T(1,128)S(1)}, s32[1,8]{1,0:T(1,128)}, u32[]{:S(2)}) copy-start(s32[1,8]{1,0:T(1,128)} %param.10) | copy-start | bytes 100
  22.1 144.7 %copy-start.3 = (s32[1,8]{1,0:T(1,128)S(1)}, s32[1,8]{1,0:T(1,128)}, u32[]{:S(2)}) copy-start(s32[1,8]{1,0:T(1,128)} %param.12) | copy-start | bytes 100
  22.1 279.5 %reduce-scatter.2.cloned.1.call-start = ((), (), s32[]{:S(2)}) async-start(), calls=%async_computation.3 | async-start | bytes 4456448 | tf_op jit(solution)/shard_map/reduce_scatter | solution.py:73
  197.4 2.2 copy-start.1
  215.9 2.2 copy-start.1
  233.2 13.5 %all-to-all-start.1 = ((bf16[16,4,2048]{2,1,0:T(4,128)(2,1)}), bf16[16,4,2048]{2,1,0:T(4,128)(2,1)S(1)}, u32[]{:S(2)}, u32[]{:S(2)}) async-start(bf16[16,4,2048]{2,1,0:T(4,128)(2,1)} %all_to_all.30), calls=%async_computation.2 | async-start | bytes 524288 | tf_op jit(solution)/shard_map/all_to_all | solution.py:80
Sparse Core Ops, SparseCore 0:
  230.5 71.0 reduce-scatter.1
where the time goes:
time: 329 us; the launch traced here: 327 us
  blocking collectives  158 us (48%)
  waiting for transfers between devices  53.3 us (16%)
  local copies, waits for them, and re-layouts  50.9 us (15%)
  other arithmetic  16.9 us (5%)
  matrix products  14.2 us (4%)
  between operations  13.5 us (4%)
  starting transfers between devices  11.1 us (3%)
  Pallas kernels  6.51 us (2%)
    all_gather x1, blocking collectives, shards(): active_lists = lax.all_gather(active, 'adapt', axis=0, tiled=True)  96.7 us
    reduce_scatter x1, waiting for transfers between devices, shards(): lax.psum_scatter(pieces.reshape(lax.axis_size('adapt') * row_count, R), '...  53.2 us
    all_gather x1, blocking collectives, shards(): lax.all_gather(lengths, 'adapt', axis=0, tiled=True)  44 us
    all_gather x1, blocking collectives, shards(): lax.all_gather(program_adapter_slot, 'adapt', axis=0, tiled=True)  17.3 us
    gather x4, local copies, waits for them, and re-layouts, one_group(): factors = down_local[group_ids]  11.2 us
    unnamed x11, local copies, waits for them, and re-layouts  8.01 us
    dot_general x1, matrix products, shards(): jnp.dot(tokens, base_weight, preferred_element_type=jnp.float32)  7.72 us
    all_to_all x1, starting transfers between devices, shards(): lax.all_to_all(tokens, 'adapt', split_axis=1, concat_axis=0, tiled=True)  7.56 us
  transfers between devices with their start and end apart: 3, of which 2 were waited for; matrix products, arithmetic and copies ran while one was open for 5% of the time, Pallas kernels for 0%

commit v1 on v0

v1 whole, which is shorter than its diff:
```python
import functools
import math

import jax
import jax.numpy as jnp
from jax import lax
from jax.experimental import pallas as pl
from jax.experimental.pallas import tpu as pltpu
from jax.sharding import PartitionSpec as P

D = 5120
KV = 512
R = 64
ACTIVE = 4
LANES = 128

adapter_scale = 2.0
MESH = pl.DeviceIdType.MESH


def kernel(
    n, down_rows, up_rows,
    active_ref, lengths_ref, slots_ref, tokens_hbm, base_hbm, store_ref, out_ref,
    tokens, base, ids_vmem, ids, send, recv, wide_weight, up_weight, total, wide,
    id_send_sem, id_recv_sem, id_sem, send_sem, recv_sem, token_sem, base_sem,
):
    me = lax.axis_index("adapt")
    d_local = 2 * down_rows
    group = LANES // math.gcd(LANES, d_local)
    groups = n // group
    half_groups = groups // 2
    span = group * d_local
    my_group, my_core = me // group, me % group
    my_half = my_group // half_groups
    row_count = out_ref.shape[0]

    token_copy = pltpu.make_async_copy(tokens_hbm, tokens, token_sem)
    base_copy = pltpu.make_async_copy(base_hbm, base, base_sem)
    token_copy.start()
    base_copy.start()

    barrier = pltpu.get_barrier_semaphore()

    def greet(k, _):
        pl.semaphore_signal(barrier, inc=1, device_id={"adapt": (me + k) % n}, device_id_type=MESH)
        return 0

    lax.fori_loop(1, n, greet, 0)
    pl.semaphore_wait(barrier, n - 1)

    def id_copy(k, origin):
        return pltpu.make_async_remote_copy(
            src_ref=active_ref, dst_ref=ids_vmem.at[origin],
            send_sem=id_send_sem.at[k], recv_sem=id_recv_sem.at[origin],
            device_id={"adapt": (me + k) % n}, device_id_type=MESH,
        )

    def send_ids(k, _):
        id_copy(k, me).start()
        return 0

    def await_ids(k, _):
        id_copy(k, (me + k) % n).wait_recv()
        return 0

    lax.fori_loop(1, n, send_ids, 0)
    ids_vmem[me] = active_ref[...]
    lax.fori_loop(1, n, await_ids, 0)
    to_scalars = pltpu.make_async_copy(ids_vmem, ids, id_sem)
    to_scalars.start()
    to_scalars.wait()

    def piece_copy(target, origin):
        return pltpu.make_async_remote_copy(
            src_ref=send.at[target], dst_ref=recv.at[origin],
            send_sem=send_sem.at[target], recv_sem=recv_sem.at[origin],
            device_id={"adapt": target}, device_id_type=MESH,
        )

    def send_group(t, _):
        other = (my_half + t + 1) % 2
        partner_group = other * half_groups + (my_group + t // 2) % half_groups

        def send_core(c, _):
            target = partner_group * group + (my_core + c) % group

            @pl.when(target != me)
            def _():
                for j in range(ACTIVE):
                    send[target, j] = store_ref[ids[target, 0, j]]
                piece_copy(target, me).start()

            return 0

        return lax.fori_loop(0, group, send_core, 0)

    lax.fori_loop(0, groups, send_group, 0)
    for j in range(ACTIVE):
        recv[me, j] = store_ref[ids[me, 0, j]]

    token_copy.wait()
    base_copy.wait()
    total[...] = jnp.zeros_like(total)
    wide[...] = jnp.zeros_like(wide)

    def base_step(g, _):
        at = pl.ds(pl.multiple_of(g * span, LANES), span)
        total[...] += jnp.dot(tokens[:, at], base[at, :], preferred_element_type=jnp.float32)
        return 0

    lax.fori_loop(0, groups, base_step, 0)

    rows = down_rows + up_rows
    twice = (
        lax.broadcasted_iota(jnp.int32, (2 * rows, rows), 0) // 2
        == lax.broadcasted_iota(jnp.int32, (2 * rows, rows), 1)
    ).astype(jnp.bfloat16)
    parity = (
        lax.broadcasted_iota(jnp.int32, (2 * rows, ACTIVE * LANES), 0) % 2
        == (lax.broadcasted_iota(jnp.int32, (2 * rows, ACTIVE * LANES), 1) % LANES) // R
    )

    def take_group(t, _):
        half = (my_half + t) % 2
        from_group = half * half_groups + (my_group - t // 2 + half_groups) % half_groups

        def take_core(c, _):
            origin = from_group * group + c

            @pl.when(origin != me)
            def _():
                piece_copy(origin, origin).wait_recv()

            packed = jnp.concatenate([recv[origin, j] for j in range(ACTIVE)], axis=1)
            spread = jnp.dot(twice, packed, preferred_element_type=jnp.float32)
            spread = jnp.where(parity, spread, 0.0)
            wide_weight[pl.ds(pl.multiple_of(c * d_local, 16), d_local), :] = spread[:d_local].astype(jnp.bfloat16)
            up_weight[pl.ds(pl.multiple_of(origin * 2 * up_rows, 8), 2 * up_rows), :] = spread[d_local:]
            return 0

        lax.fori_loop(0, group, take_core, 0)
        at = pl.ds(pl.multiple_of(from_group * span, LANES), span)
        wide[...] += jnp.dot(tokens[:, at], wide_weight[...], preferred_element_type=jnp.float32)
        return 0

    lax.fori_loop(0, groups, take_group, 0)

    position = lax.broadcasted_iota(jnp.int32, (row_count, LANES), 0)
    row_slot = jnp.zeros((row_count, LANES), jnp.int32)
    begin = jnp.int32(0)
    for p in range(lengths_ref.shape[1]):
        end = begin + lengths_ref[0, p]
        inside = jnp.logical_and(position >= begin, position < end)
        row_slot = jnp.where(inside, slots_ref[0, p], row_slot)
        begin = end
    picked = []
    for j in range(ACTIVE):
        mine = wide[:, j * LANES:(j + 1) * LANES]
        low = mine + pltpu.roll(mine, R, 1)
        picked.append(jnp.where(row_slot == j, low, 0.0).astype(jnp.bfloat16))
    low_rank = jnp.concatenate(picked, axis=1)
    delta = lax.dot_general(
        low_rank, up_weight[...].astype(jnp.bfloat16),
        (((1,), (1,)), ((), ())), preferred_element_type=jnp.float32,
    )
    out_ref[...] = (total[...] + adapter_scale * delta).astype(out_ref.dtype)

    def finish(k, _):
        target = (me + k) % n
        id_copy(k, me).wait_send()
        piece_copy(target, me).wait_send()
        return 0

    lax.fori_loop(1, n, finish, 0)


def shards(tokens, lengths, active, program_adapter_slot, base_weight, adapter_down, adapter_up):
    n = lax.axis_size("adapt")
    row_count = tokens.shape[0]
    stored = adapter_down.shape[0]
    down_rows = adapter_down.shape[1] // LANES
    up_rows = adapter_up.shape[1] // LANES
    rows = down_rows + up_rows
    store = jnp.concatenate([adapter_down, adapter_up], axis=1).reshape(stored, rows, LANES)
    slot_list = jnp.pad(active, ((0, 0), (0, LANES - ACTIVE)))
    d_local = 2 * down_rows
    group = LANES // math.gcd(LANES, d_local)
    vmem, smem, hbm = pltpu.VMEM, pltpu.SMEM, pl.ANY
    width = ACTIVE * LANES
    return pl.pallas_call(
        functools.partial(kernel, n, down_rows, up_rows),
        out_shape=jax.ShapeDtypeStruct((row_count, KV), jnp.bfloat16),
        in_specs=[pl.BlockSpec(memory_space=s) for s in (vmem, smem, smem, hbm, hbm, vmem)],
        out_specs=pl.BlockSpec(memory_space=vmem),
        scratch_shapes=[
            pltpu.VMEM((row_count, D), jnp.bfloat16),
            pltpu.VMEM((D, KV), jnp.bfloat16),
            pltpu.VMEM((n, 1, LANES), jnp.int32),
            pltpu.SMEM((n, 1, LANES), jnp.int32),
            pltpu.VMEM((n, ACTIVE, rows, LANES), jnp.bfloat16),
            pltpu.VMEM((n, ACTIVE, rows, LANES), jnp.bfloat16),
            pltpu.VMEM((group * d_local, width), jnp.bfloat16),
            pltpu.VMEM((KV, width), jnp.float32),
            pltpu.VMEM((row_count, KV), jnp.float32),
            pltpu.VMEM((row_count, width), jnp.float32),
            pltpu.SemaphoreType.DMA((n,)),
            pltpu.SemaphoreType.DMA((n,)),
            pltpu.SemaphoreType.DMA,
            pltpu.SemaphoreType.DMA((n,)),
            pltpu.SemaphoreType.DMA((n,)),
            pltpu.SemaphoreType.DMA,
            pltpu.SemaphoreType.DMA,
        ],
        compiler_params=pltpu.CompilerParams(
            collective_id=0, has_side_effects=True, vmem_limit_bytes=48 * 1024 * 1024
        ),
    )(slot_list, lengths, program_adapter_slot, tokens, base_weight, store)


def solution(mesh):
    in_specs = (
        P(("groups", "adapt"), None),
        P(("groups", "adapt"), None),
        P(("groups", "adapt"), None),
        P(("groups", "adapt"), None),
        P(),
        P("groups", "adapt"),
        P("groups", "adapt"),
    )
    out_specs = P(("groups", "adapt"), None)
    return jax.shard_map(shards, mesh=mesh, in_specs=in_specs, out_specs=out_specs, check_vma=False)
```

time: 329 us -> 80.3 us (0.24)
  blocking collectives: 158 us -> 0 us
  Pallas kernels: 6.51 us -> 76.7 us
  waiting for transfers between devices: 53.3 us -> 0 us
  local copies, waits for them, and re-layouts: 50.9 us -> 1.45 us
  other arithmetic: 16.9 us -> 1.49 us
  matrix products: 14.2 us -> 0 us
  between operations: 13.5 us -> 0.05 us
  starting transfers between devices: 11.1 us -> 0 us
    all_gather x3 -> x0, blocking collectives: 158 us -> none  [the longest x1 96.7 us: shards(): active_lists = lax.all_gather(active, 'adapt', axis=0, tiled=True)]
    pallas_call x0 -> x1, Pallas kernels: none -> 76.7 us  [shards(): pl.pallas_call(functools.partial(kernel, n, down_rows, up_rows), out_shap...]
    reduce_scatter x1 -> x0, waiting for transfers between devices: 53.2 us -> none  [shards(): lax.psum_scatter(pieces.reshape(lax.axis_size('adapt') * row_count, R), '...]
    gather x7 -> x0, local copies, waits for them, and re-layouts: 17.1 us -> none  [the longest x4 11.2 us: one_group(): factors = down_local[group_ids]]
    all_to_all x2 -> x0, starting transfers between devices: 11.1 us -> none  [the longest x1 7.56 us: shards(): lax.all_to_all(tokens, 'adapt', split_axis=1, concat_axis=0, tiled=True)]
    dot_general x1 -> x0, matrix products: 7.72 us -> none  [shards(): jnp.dot(tokens, base_weight, preferred_element_type=jnp.float32)]
    sort x2 -> x0, other arithmetic: 7.56 us -> none  [the longest x1 3.78 us: shards(): order = jnp.argsort(row_slot, stable=True)]
    reduce_sum x9 -> x0, other arithmetic: 7.12 us -> none  [the longest x2 5.87 us: one_group(): jnp.sum(picks[:, :, :, None] * wide, axis=2)]
  transfers between devices with their start and end apart: 3 -> 0, of which waited for: 2 -> 0; matrix products, arithmetic and copies ran while one was open for 5% -> 0% of each run, Pallas kernels for 0% -> 0%
where the time goes in v1:
time: 80.3 us; the launch traced here: 79.7 us
  Pallas kernels  76.7 us (96%)
  other arithmetic  1.49 us (2%)
  local copies, waits for them, and re-layouts  1.45 us (2%)
    pallas_call x1, Pallas kernels, shards(): pl.pallas_call(functools.partial(kernel, n, down_rows, up_rows), out_shap...  76.7 us

profile of v1, /device:TPU:0, one launch (start us, length us, event | category | flops | bytes accessed | tf_op | source)
XLA Modules:
  0.0 79.7 jit_solution(8288608801320595684)
XLA Ops:
  0.0 1.5 %maximum_bitcast_fusion = bf16[4,8,176,128]{3,1,2,0:T(8,128)(2,1)S(1)} fusion(bf16[32,2048]{1,0:T(8,128)(2,1)} %param.13, bf16[32,20480]{1,0:T(8,128)(2,1)} %param.12), kind=kLoop, calls=%fused_computation | loop fusion | flops 2883584 | bytes 2883584
  1.5 0.0 copy-start.2
  1.5 0.0 copy-start
  1.5 0.0 copy-start.1
  1.5 0.2 copy.8
  1.7 0.4 copy-done.2
  2.2 0.0 copy-done
  2.2 0.0 copy-done.1
  2.2 76.7 %shard_map.73 = bf16[512,512]{1,0:T(8,128)(2,1)S(1)} custom-call(s32[1,128]{1,0:T(1,128)S(1)} %pad.4.active_ref, s32[1,8]{1,0:T(1,128)S(1)} %copy-done, s32[1,8]{1,0:T(1,128)S(1)} %copy-done.1, bf16[512,5120]{1,0:T(8,128)(2,1)} %tokens_hbm.1, bf16[5120,512]{1,0:T(8,128)(2,1)} %base_hbm.1, bf16[32,176,128]{2,1,0:T(8,128)(2,1)S(1)} %bitcast.3), custom_call_target="tpu_custom_call" | custom-call | tf_op jit(solution)/shard_map/pallas_call | solution.py:190
  78.9 0.8 copy.10
  (1 shorter events, 0.0 us)
Async XLA Ops:
  1.5 0.7 copy-start.2
  1.5 0.7 copy-start
  1.5 0.7 copy-start.1

commit v2 on v1

--- a/solution.py
+++ b/solution.py
@@ -18,7 +18,7 @@
 MESH = pl.DeviceIdType.MESH
 
 
-def kernel(
+def direct_kernel(
     n, down_rows, up_rows,
     active_ref, lengths_ref, slots_ref, tokens_hbm, base_hbm, store_ref, out_ref,
     tokens, base, ids_vmem, ids, send, recv, wide_weight, up_weight, total, wide,
@@ -174,21 +174,355 @@
     lax.fori_loop(1, n, finish, 0)
 
 
-def shards(tokens, lengths, active, program_adapter_slot, base_weight, adapter_down, adapter_up):
+def chunks_of(tiles):
+    bounds, at = [], 0
+    for size in (3, 2, 2, 2, 1, 1):
+        if at < tiles:
+            bounds.append((at, min(tiles, at + size)))
+            at += size
+    if at < tiles:
+        bounds.append((at, tiles))
+    return bounds
+
+
+def running_sum(counts):
+    lane = lax.broadcasted_iota(jnp.int32, counts.shape, 1)
+    shift = 1
+    while shift < LANES:
+        counts = counts + jnp.where(lane >= shift, pltpu.roll(counts, shift, 1), 0)
+        shift *= 2
+    return counts
+
+
+def relay_kernel(
+    n, part_count, down_rows, up_rows, capacity,
+    active_ref, lengths_ref, slots_ref, tokens_hbm, base_hbm, store_ref, out_ref, flag_ref,
+    tokens, base, ids_vmem, ids, place_vmem, place, list_vmem, id_list,
+    far_send, send, recv, wide_weight, far_weight, up_weight, total, wide, flags, my_flag,
+    id_send_sem, id_recv_sem, scalar_sem, far_send_sem, far_recv_sem, send_sem, own_send_sem, recv_sem,
+    token_sem, base_sem, flag_send_sem, flag_recv_sem, *far,
+):
+    me = lax.axis_index("adapt")
+    part = lax.axis_index("groups")
+    d_local = 2 * down_rows
+    rows = down_rows + up_rows
+    tiles = store_ref.shape[0]
+    pieces = chunks_of(tiles)
+    half_n = n // 2
+    plane_n = n // 4
+    half = me // half_n
+    other = 1 - half
+    plane, within = me // plane_n, me % plane_n
+    relays = plane == 1 + half
+    relay_target = (1 + other) * plane_n + within
+    group = LANES // math.gcd(LANES, d_local)
+    half_groups = half_n // group
+    span = group * d_local
+    row_count = out_ref.shape[0]
+
+    token_copy = pltpu.make_async_copy(tokens_hbm, tokens, token_sem)
+    base_copy = pltpu.make_async_copy(base_hbm, base, base_sem)
+    token_copy.start()
+    base_copy.start()
+
+    barrier = pltpu.get_barrier_semaphore()
+
+    def greet(k, _):
+        pl.semaphore_signal(
+            barrier, inc=1, device_id={"groups": part, "adapt": (me + k) % n}, device_id_type=MESH)
+        return 0
+
+    def greet_part(k, _):
+        pl.semaphore_signal(
+            barrier, inc=1, device_id={"groups": (part + k) % part_count, "adapt": me}, device_id_type=MESH)
+        return 0
+
+    lax.fori_loop(1, n, greet, 0)
+    lax.fori_loop(1, part_count, greet_part, 0)
+    pl.semaphore_wait(barrier, n - 1 + part_count - 1)
+
+    def id_copy(k, origin):
+        return pltpu.make_async_remote_copy(
+            src_ref=active_ref, dst_ref=ids_vmem.at[origin],
+            send_sem=id_send_sem.at[k], recv_sem=id_recv_sem.at[origin],
+            device_id={"groups": part, "adapt": (me + k) % n}, device_id_type=MESH,
+        )
+
+    def send_ids(k, _):
+        id_copy(k, me).start()
+        return 0
+
+    def await_ids(k, _):
+        id_copy(k, (me + k) % n).wait_recv()
+        return 0
+
+    lax.fori_loop(1, n, send_ids, 0)
+    ids_vmem[me] = active_ref[...]
+    lax.fori_loop(1, n, await_ids, 0)
+
+    def ranks(which):
+        theirs = ids_vmem[pl.ds(which * half_n, half_n)].reshape(half_n * 8, LANES)
+        lane = lax.broadcasted_iota(jnp.int32, theirs.shape, 1)
+        hit = (theirs == lane).astype(jnp.int32)
+        present = jnp.broadcast_to(jnp.max(hit, axis=0, keepdims=True), (8, LANES))
+        through = running_sum(present)
+        return hit, present, through - present, jnp.max(through, axis=1, keepdims=True)
+
+    _, far_present, far_rank, far_count = ranks(other)
+    order = lax.broadcasted_iota(jnp.int32, (capacity, LANES), 0)
+    number = lax.broadcasted_iota(jnp.int32, (capacity, LANES), 1)
+    chosen = jnp.where((far_rank[0:1] == order) & (far_present[0:1] > 0), number, 0)
+    list_vmem[...] = jnp.broadcast_to(jnp.sum(chosen, axis=1, keepdims=True), (capacity, LANES))
+    hit, _, near_rank, near_count = ranks(half)
+    spot = jnp.minimum(jnp.sum(hit * near_rank[0:1], axis=1, keepdims=True), capacity - 1)
+    place_vmem[...] = jnp.broadcast_to(spot, (half_n * 8, LANES))
+    my_flag[...] = jnp.broadcast_to(
+        (jnp.maximum(far_count, near_count) > capacity).astype(jnp.int32), (8, LANES))
+
+    scalar_copies = [
+        pltpu.make_async_copy(list_vmem, id_list, scalar_sem.at[0]),
+        pltpu.make_async_copy(ids_vmem, ids, scalar_sem.at[1]),
+        pltpu.make_async_copy(place_vmem, place, scalar_sem.at[2]),
+    ]
+    for copy in scalar_copies:
+        copy.start()
+    for copy in scalar_copies:
+        copy.wait()
+
+    def far_copy(q, slot):
+        low, high = pieces[q]
+        return pltpu.make_async_remote_copy(
+            src_ref=far_send.at[pl.ds(low, high - low)], dst_ref=far[q].at[slot],
+            send_sem=far_send_sem.at[q], recv_sem=far_recv_sem.at[slot, q],
+            device_id={"groups": part, "adapt": relay_target}, device_id_type=MESH,
+        )
+
+    for q, (low, high) in enumerate(pieces):
+        def fill(k, _):
+            for t in range(low, high):
+                far_send[t, k] = store_ref[t, id_list[k, 0]]
+            return 0
+
+        lax.fori_loop(0, capacity, fill, 0)
+        far_copy(q, plane % 2).start()
+
+    def own_copy(d, origin):
+        return pltpu.make_async_remote_copy(
+            src_ref=send.at[2, d], dst_ref=recv.at[origin],
+            send_sem=own_send_sem.at[d], recv_sem=recv_sem.at[origin, 0],
+            device_id={"groups": part, "adapt": half * half_n + d}, device_id_type=MESH,
+        )
+
+    def send_own(k, _):
+        d = (me + k) % half_n
+        target = half * half_n + d
+        for j in range(ACTIVE):
+            for t in range(tiles):
+                send[2, d, t, j] = store_ref[t, ids[target, j, 0]]
+        own_copy(d, me).start()
+        return 0
+
+    lax.fori_loop(1, half_n, send_own, 0)
+    for j in range(ACTIVE):
+        for t in range(tiles):
+            recv[me, t, j] = store_ref[t, ids[me, j, 0]]
+
+    def part_copy(q, f, d, origin):
+        low, high = pieces[q]
+        return pltpu.make_async_remote_copy(
+            src_ref=send.at[f, d, pl.ds(low, high - low)], dst_ref=recv.at[origin, pl.ds(low, high - low)],
+            send_sem=send_sem.at[f, d, q], recv_sem=recv_sem.at[origin, q],
+            device_id={"groups": part, "adapt": half * half_n + d}, device_id_type=MESH,
+        )
+
+    def far_origin(f):
+        return (2 * other + f) * plane_n + within
+
+    def relay(q):
+        low, high = pieces[q]
+        for f in range(2):
+            far_copy(q, f).wait_recv()
+        for f in range(2):
+            def pass_on(k, _):
+                d = (me + k) % half_n
+                for j in range(ACTIVE):
+                    for t in range(low, high):
+                        send[f, d, t, j] = far[q][f, t - low, place[d * 8 + j, 0]]
+                part_copy(q, f, d, far_origin(f)).start()
+                return 0
+
+            lax.fori_loop(1, half_n, pass_on, 0)
+            for j in range(ACTIVE):
+                for t in range(low, high):
+                    recv[far_origin(f), t, j] = far[q][f, t - low, place[(me % half_n) * 8 + j, 0]]
+
+    def spread_rows(origin, low, high):
+        count = (high - low) * 16
+        packed = jnp.concatenate(
+            [recv[origin, low:high, j].reshape(count, LANES) for j in range(ACTIVE)], axis=1)
+        twice = (
+            lax.broadcasted_iota(jnp.int32, (2 * count, count), 0) // 2
+            == lax.broadcasted_iota(jnp.int32, (2 * count, count), 1)
+        ).astype(jnp.bfloat16)
+        parity = (
+            lax.broadcasted_iota(jnp.int32, (2 * count, ACTIVE * LANES), 0) % 2
+            == (lax.broadcasted_iota(jnp.int32, (2 * count, ACTIVE * LANES), 1) % LANES) // R
+        )
+        return jnp.where(parity, jnp.dot(twice, packed, preferred_element_type=jnp.float32), 0.0)
+
+    def place_rows(origin, low, high, target, offset):
+        spread = spread_rows(origin, low, high)
+        first, last = 32 * low, 32 * high
+        if first < d_local:
+            here = min(last, d_local) - first
+            at = pl.ds(pl.multiple_of(offset + first, 16), here)
+            target[at, :] = spread[:here].astype(jnp.bfloat16)
+        if last > d_local:
+            begin = max(first, d_local)
+            end = min(last, 2 * rows)
+            at = pl.ds(pl.multiple_of(origin * 2 * up_rows + begin - d_local, 8), end - begin)
+            up_weight[at, :] = spread[begin - first:end - first]
+
+    def base_step(g, _):
+        at = pl.ds(pl.multiple_of(g * span, LANES), span)
+        total[...] += jnp.dot(tokens[:, at], base[at, :], preferred_element_type=jnp.float32)
+        return 0
+
+    def near_step(g, _):
+        from_group = half * half_groups + (me % half_n // group + g) % half_groups
+
+        def take_core(c, _):
+            origin = from_group * group + c
+
+            @pl.when(origin != me)
+            def _():
+                own_copy(me % half_n, origin).wait_recv()
+
+            place_rows(origin, 0, tiles, wide_weight, c * d_local)
+            return 0
+
+        lax.fori_loop(0, group, take_core, 0)
+        at = pl.ds(pl.multiple_of(from_group * span, LANES), span)
+        wide[...] += jnp.dot(tokens[:, at], wide_weight[...], preferred_element_type=jnp.float32)
+        return 0
+
+    def take_far(q):
+        low, high = pieces[q]
+
+        def take_one(k, _):
+            origin = other * half_n + k
+            passed = (1 + half) * plane_n + k % plane_n
+
+            @pl.when(passed != me)
+            def _():
+                part_copy(q, 0, me % half_n, origin).wait_recv()
+
+            place_rows(origin, low, high, far_weight, k * d_local)
+            return 0
+
+        lax.fori_loop(0, half_n, take_one, 0)
+
+    token_copy.wait()
+    base_copy.wait()
+    total[...] = jnp.zeros_like(total)
+    wide[...] = jnp.zeros_like(wide)
+    steps = len(pieces)
+    for q in range(steps):
+        @pl.when(relays)
+        def _():
+            relay(q)
+
+        low, high = 2 * half_groups * q // steps, 2 * half_groups * (q + 1) // steps
+        lax.fori_loop(low, high, base_step, 0)
+        low, high = half_groups * q // steps, half_groups * (q + 1) // steps
+        lax.fori_loop(low, high, near_step, 0)
+        if q >= 1:
+            take_far(q - 1)
+    take_far(steps - 1)
+
+    def far_step(g, _):
+        at = pl.ds(pl.multiple_of(other * half_n * d_local + g * span, LANES), span)
+        of = pl.ds(pl.multiple_of(g * span, LANES), span)
+        wide[...] += jnp.dot(tokens[:, at], far_weight[of, :], preferred_element_type=jnp.float32)
+        return 0
+
+    lax.fori_loop(0, half_groups, far_step, 0)
+
+    position = lax.broadcasted_iota(jnp.int32, (row_count, LANES), 0)
+    row_slot = jnp.zeros((row_count, LANES), jnp.int32)
+    begin = jnp.int32(0)
+    for p in range(lengths_ref.shape[1]):
+        end = begin + lengths_ref[0, p]
+        inside = jnp.logical_and(position >= begin, position < end)
+        row_slot = jnp.where(inside, slots_ref[0, p], row_slot)
+        begin = end
+    picked = []
+    for j in range(ACTIVE):
+        mine = wide[:, j * LANES:(j + 1) * LANES]
+        low_rank = mine + pltpu.roll(mine, R, 1)
+        picked.append(jnp.where(row_slot == j, low_rank, 0.0).astype(jnp.bfloat16))
+    delta = lax.dot_general(
+        jnp.concatenate(picked, axis=1), up_weight[...].astype(jnp.bfloat16),
+        (((1,), (1,)), ((), ())), preferred_element_type=jnp.float32,
+    )
+    out_ref[...] = (total[...] + adapter_scale * delta).astype(out_ref.dtype)
+
+    def flag_copy(k, origin):
+        return pltpu.make_async_remote_copy(
+            src_ref=my_flag, dst_ref=flags.at[origin],
+            send_sem=flag_send_sem.at[k], recv_sem=flag_recv_sem.at[origin],
+            device_id={"groups": (part + k) % part_count, "adapt": me}, device_id_type=MESH,
+        )
+
+    def send_flag(k, _):
+        flag_copy(k, part).start()
+        return 0
+
+    def await_flag(k, _):
+        flag_copy(k, (part + k) % part_count).wait_recv()
+        flag_copy(k, part).wait_send()
+        return 0
+
+    lax.fori_loop(1, part_count, send_flag, 0)
+    flags[part] = my_flag[...]
+
+    def finish(k, _):
+        id_copy(k, me).wait_send()
+        return 0
+
+    def finish_near(k, _):
+        own_copy((me + k) % half_n, me).wait_send()
+        return 0
+
+    lax.fori_loop(1, n, finish, 0)
+    lax.fori_loop(1, half_n, finish_near, 0)
+    for q in range(steps):
+        far_copy(q, plane % 2).wait_send()
+
+    @pl.when(relays)
+    def _():
+        for q in range(steps):
+            for f in range(2):
+                def finish_part(k, _):
+                    part_copy(q, f, (me + k) % half_n, far_origin(f)).wait_send()
+                    return 0
+
+                lax.fori_loop(1, half_n, finish_part, 0)
+
+    lax.fori_loop(1, part_count, await_flag, 0)
+    flag_ref[...] = jnp.max(flags[...], axis=0)
+
+
+def direct(slot_list, lengths, program_adapter_slot, tokens, base_weight, store, down_rows, up_rows):
     n = lax.axis_size("adapt")
     row_count = tokens.shape[0]
-    stored = adapter_down.shape[0]
-    down_rows = adapter_down.shape[1] // LANES
-    up_rows = adapter_up.shape[1] // LANES
     rows = down_rows + up_rows
-    store = jnp.concatenate([adapter_down, adapter_up], axis=1).reshape(stored, rows, LANES)
-    slot_list = jnp.pad(active, ((0, 0), (0, LANES - ACTIVE)))
     d_local = 2 * down_rows
     group = LANES // math.gcd(LANES, d_local)
     vmem, smem, hbm = pltpu.VMEM, pltpu.SMEM, pl.ANY
     width = ACTIVE * LANES
     return pl.pallas_call(
-        functools.partial(kernel, n, down_rows, up_rows),
+        functools.partial(direct_kernel, n, down_rows, up_rows),
         out_shape=jax.ShapeDtypeStruct((row_count, KV), jnp.bfloat16),
         in_specs=[pl.BlockSpec(memory_space=s) for s in (vmem, smem, smem, hbm, hbm, vmem)],
         out_specs=pl.BlockSpec(memory_space=vmem),
@@ -212,9 +546,79 @@
             pltpu.SemaphoreType.DMA,
         ],
         compiler_params=pltpu.CompilerParams(
-            collective_id=0, has_side_effects=True, vmem_limit_bytes=48 * 1024 * 1024
+            collective_id=1, has_side_effects=True, vmem_limit_bytes=48 * 1024 * 1024
         ),
     )(slot_list, lengths, program_adapter_slot, tokens, base_weight, store)
+
+
+def shards(tokens, lengths, active, program_adapter_slot, base_weight, adapter_down, adapter_up):
+    n = lax.axis_size("adapt")
+    part_count = lax.axis_size("groups")
+    row_count = tokens.shape[0]
+    stored = adapter_down.shape[0]
+    down_rows = adapter_down.shape[1] // LANES
+    up_rows = adapter_up.shape[1] // LANES
+    rows = down_rows + up_rows
+    tiles = -(-rows // 16)
+    both = jnp.concatenate([adapter_down, adapter_up], axis=1)
+    store = jnp.pad(both, ((0, 0), (0, (16 * tiles - rows) * LANES)))
+    store = store.reshape(stored, tiles, 16, LANES).transpose(1, 0, 2, 3)
+    slot_rows = jnp.broadcast_to(active.reshape(ACTIVE, 1), (ACTIVE, LANES))
+    slot_rows = jnp.pad(slot_rows, ((0, 8 - ACTIVE), (0, 0)), constant_values=-1)
+    d_local = 2 * down_rows
+    group = LANES // math.gcd(LANES, d_local)
+    half_n = n // 2
+    capacity = 3 * min(stored, half_n * ACTIVE) // 4
+    steps = len(chunks_of(tiles))
+    width = ACTIVE * LANES
+    vmem, smem, hbm = pltpu.VMEM, pltpu.SMEM, pl.ANY
+    dma = pltpu.SemaphoreType.DMA
+    values, flag = pl.pallas_call(
+        functools.partial(relay_kernel, n, part_count, down_rows, up_rows, capacity),
+        out_shape=(
+            jax.ShapeDtypeStruct((row_count, KV), jnp.bfloat16),
+            jax.ShapeDtypeStruct((8, LANES), jnp.int32),
+        ),
+        in_specs=[pl.BlockSpec(memory_space=s) for s in (vmem, smem, smem, hbm, hbm, vmem)],
+        out_specs=(pl.BlockSpec(memory_space=vmem), pl.BlockSpec(memory_space=vmem)),
+        scratch_shapes=[
+            pltpu.VMEM((row_count, D), jnp.bfloat16),
+            pltpu.VMEM((D, KV), jnp.bfloat16),
+            pltpu.VMEM((n, 8, LANES), jnp.int32),
+            pltpu.SMEM((n, 8, LANES), jnp.int32),
+            pltpu.VMEM((half_n * 8, LANES), jnp.int32),
+            pltpu.SMEM((half_n * 8, LANES), jnp.int32),
+            pltpu.VMEM((capacity, LANES), jnp.int32),
+            pltpu.SMEM((capacity, LANES), jnp.int32),
+            pltpu.VMEM((tiles, capacity, 16, LANES), jnp.bfloat16),
+            pltpu.VMEM((3, half_n, tiles, ACTIVE, 16, LANES), jnp.bfloat16),
+            pltpu.VMEM((n, tiles, ACTIVE, 16, LANES), jnp.bfloat16),
+            pltpu.VMEM((group * d_local, width), jnp.bfloat16),
+            pltpu.VMEM((half_n * d_local, width), jnp.bfloat16),
+            pltpu.VMEM((KV, width), jnp.float32),
+            pltpu.VMEM((row_count, KV), jnp.float32),
+            pltpu.VMEM((row_count, width), jnp.float32),
+            pltpu.VMEM((part_count, 8, LANES), jnp.int32),
+            pltpu.VMEM((8, LANES), jnp.int32),
+            dma((n,)), dma((n,)), dma((3,)), dma((steps,)), dma((2, steps)),
+            dma((2, half_n, steps)), dma((half_n,)), dma((n, steps)),
+            dma, dma, dma((part_count,)), dma((part_count,)),
+        ] + [
+            pltpu.VMEM((2, high - low, capacity, 16, LANES), jnp.bfloat16)
+            for low, high in chunks_of(tiles)
+        ],
+        compiler_params=pltpu.CompilerParams(
+            collective_id=0, has_side_effects=True, vmem_limit_bytes=56 * 1024 * 1024
+        ),
+    )(slot_rows, lengths, program_adapter_slot, tokens, base_weight, store)
+
+    def over(_):
+        slot_list = jnp.pad(active, ((0, 0), (0, LANES - ACTIVE)))
+        return direct(
+            slot_list, lengths, program_adapter_slot, tokens, base_weight,
+            both.reshape(stored, rows, LANES), down_rows, up_rows)
+
+    return lax.cond(flag[0, 0] > 0, over, lambda ready: ready, values)
 
 
 def solution(mesh):

time: 80.3 us -> 94.6 us (1.18)
  Pallas kernels: 76.7 us -> 87.2 us
  local copies, waits for them, and re-layouts: 1.45 us -> 6.42 us
  other arithmetic: 1.49 us -> 0 us
    pallas_call x1, Pallas kernels: 76.7 us -> 87.2 us  [shards(): pl.pallas_call(functools.partial(relay_kernel, n, part_count, down_rows,...]
    unnamed x8 -> x13, local copies, waits for them, and re-layouts: 1.45 us -> 3.12 us
    unnamed x1 -> x0, other arithmetic: 1.49 us -> none
    reshape x0 -> x1, local copies, waits for them, and re-layouts: none -> 1.44 us  [shards(): store = store.reshape(stored, tiles, 16, LANES).transpose(1, 0, 2, 3)]
    slice x0 -> x1, local copies, waits for them, and re-layouts: none -> 1.19 us  [shards(): return lax.cond(flag[0, 0] > 0, over, lambda ready: ready, values)]
where the time goes in v2:
time: 94.6 us; the launch traced here: 94.4 us
  Pallas kernels  87.2 us (92%)
  local copies, waits for them, and re-layouts  6.42 us (7%)
    pallas_call x1, Pallas kernels, shards(): pl.pallas_call(functools.partial(relay_kernel, n, part_count, down_rows,...  87.2 us
    unnamed x13, local copies, waits for them, and re-layouts  3.12 us

profile of v2, /device:TPU:0, one launch (start us, length us, event | category | flops | bytes accessed | tf_op | source)
XLA Modules:
  0.0 94.4 jit_solution(3361180857717486525)
XLA Ops:
  0.0 0.0 copy-start.1
  0.0 1.4 %constant_dynamic-update-slice_fusion.1 = bf16[32,22528]{1,0:T(8,128)(2,1)S(1)} fusion(bf16[32,20480]{1,0:T(8,128)(2,1)} %param.14), kind=kLoop, calls=%fused_computation.2 | loop fusion | bytes 2621440
  1.4 0.0 copy-done.1
  1.5 0.0 copy-start
  1.5 0.2 copy.12
  1.7 0.0 copy-start.4
  1.7 0.0 copy-start.2
  1.7 0.0 copy-start.3
  1.7 1.4 %copy.14 = bf16[32,11,16,128]{3,2,0,1:T(8,128)(2,1)} copy(bf16[32,11,16,128]{3,2,1,0:T(8,128)(2,1)S(1)} %bitcast.13) | data formatting | bytes 2883584 | tf_op jit(solution)/shard_map/reshape | solution.py:565
  3.2 0.0 copy-done.4
  3.2 0.7 pad.11.active_ref
  3.8 0.7 copy-done
  4.5 0.0 copy-done.2
  4.5 0.0 copy-done.3
  4.5 87.2 %shard_map.75 = (bf16[512,512]{1,0:T(8,128)(2,1)S(1)}, s32[8,128]{1,0:T(8,128)}) custom-call(s32[8,128]{1,0:T(8,128)} %pad.11.active_ref, s32[1,8]{1,0:T(1,128)S(1)} %copy-done.2, s32[1,8]{1,0:T(1,128)S(1)} %copy-done.3, bf16[512,5120]{1,0:T(8,128)(2,1)S(1)} %copy-done, bf16[5120,512]{1,0:T(8,128)(2,1)} %base_hbm.1, bf16[11,32,16,128]{3,2,1,0:T(8,128)(2,1)} %bitcast.14), custom_call_target="tpu_custom_call" | custom-call | tf_op jit(solution)/shard_map/pallas_call | solution.py:576
  91.7 1.2 %slice.3 = s32[1,1]{1,0:T(1,128)} slice(s32[8,128]{1,0:T(8,128)} %get-tuple-element.29), slice={[0:1], [0:1]} | slice | bytes 8 | tf_op jit(solution)/shard_map/slice | solution.py:621
  93.6 0.8 copy.19
  (3 shorter events, 0.0 us)
Async XLA Ops:
  0.0 1.4 %copy-start.1 = (bf16[32,2048]{1,0:T(8,128)(2,1)S(1)}, bf16[32,2048]{1,0:T(8,128)(2,1)}, u32[]{:S(2)}) copy-start(bf16[32,2048]{1,0:T(8,128)(2,1)} %param.15) | copy-start | bytes 393220
  1.5 3.0 %copy-start = (bf16[512,5120]{1,0:T(8,128)(2,1)S(1)}, bf16[512,5120]{1,0:T(8,128)(2,1)}, u32[]{:S(2)}) copy-start(bf16[512,5120]{1,0:T(8,128)(2,1)} %tokens_hbm.1) | copy-start | bytes 15728644
  1.7 1.5 %copy-start.4 = (s32[1,4]{1,0:T(1,128)S(1)}, s32[1,4]{1,0:T(1,128)}, u32[]{:S(2)}) copy-start(s32[1,4]{1,0:T(1,128)} %param.11) | copy-start | bytes 52
  1.7 2.8 %copy-start.2 = (s32[1,8]{1,0:T(1,128)S(1)}, s32[1,8]{1,0:T(1,128)}, u32[]{:S(2)}) copy-start(s32[1,8]{1,0:T(1,128)} %lengths_ref.1) | copy-start | bytes 100
  1.7 2.8 %copy-start.3 = (s32[1,8]{1,0:T(1,128)S(1)}, s32[1,8]{1,0:T(1,128)}, u32[]{:S(2)}) copy-start(s32[1,8]{1,0:T(1,128)} %slots_ref.1) | copy-start | bytes 100

commit v3 on v1

--- a/solution.py
+++ b/solution.py
@@ -88,6 +88,9 @@
             def _():
                 for j in range(ACTIVE):
                     send[target, j] = store_ref[ids[target, 0, j]]
+
+            @pl.when(jnp.logical_and(target != me, jnp.logical_or(t % 2 == 1, t < 4)))
+            def _():
                 piece_copy(target, me).start()
 
             return 0
@@ -143,7 +146,32 @@
         wide[...] += jnp.dot(tokens[:, at], wide_weight[...], preferred_element_type=jnp.float32)
         return 0
 
-    lax.fori_loop(0, groups, take_group, 0)
+    def far_target(q, c):
+        partner_group = (1 - my_half) * half_groups + (my_group + q) % half_groups
+        return partner_group * group + (my_core + c) % group
+
+    def take_near(q, _):
+        return take_group(2 * q, 0)
+
+    def take_far(q, _):
+        def sent(c, _):
+            piece_copy(far_target(q, c), me).wait_send()
+            return 0
+
+        def start_later(c, _):
+            piece_copy(far_target(q + 2, c), me).start()
+            return 0
+
+        lax.fori_loop(0, group, sent, 0)
+
+        @pl.when(q + 2 < half_groups)
+        def _():
+            lax.fori_loop(0, group, start_later, 0)
+
+        return take_group(2 * q + 1, 0)
+
+    lax.fori_loop(0, half_groups, take_near, 0)
+    lax.fori_loop(0, half_groups, take_far, 0)
 
     position = lax.broadcasted_iota(jnp.int32, (row_count, LANES), 0)
     row_slot = jnp.zeros((row_count, LANES), jnp.int32)
@@ -166,12 +194,16 @@
     out_ref[...] = (total[...] + adapter_scale * delta).astype(out_ref.dtype)
 
     def finish(k, _):
-        target = (me + k) % n
         id_copy(k, me).wait_send()
-        piece_copy(target, me).wait_send()
+        return 0
+
+    def finish_near(k, _):
+        half_n = n // 2
+        piece_copy(my_half * half_n + (me + k) % half_n, me).wait_send()
         return 0
 
     lax.fori_loop(1, n, finish, 0)
+    lax.fori_loop(1, n // 2, finish_near, 0)
 
 
 def shards(tokens, lengths, active, program_adapter_slot, base_weight, adapter_down, adapter_up):

time: 80.3 us -> 84.8 us (1.056)
  Pallas kernels: 76.7 us -> 81.6 us
    pallas_call x1, Pallas kernels: 76.7 us -> 81.6 us  [shards(): pl.pallas_call(functools.partial(kernel, n, down_rows, up_rows), out_shap...]
where the time goes in v3:
time: 84.8 us; the launch traced here: 84.6 us
  Pallas kernels  81.6 us (96%)
  other arithmetic  1.49 us (2%)
  local copies, waits for them, and re-layouts  1.45 us (2%)
    pallas_call x1, Pallas kernels, shards(): pl.pallas_call(functools.partial(kernel, n, down_rows, up_rows), out_shap...  81.6 us

profile of v3, /device:TPU:0, one launch (start us, length us, event | category | flops | bytes accessed | tf_op | source)
XLA Modules:
  0.0 84.6 jit_solution(8890352542008361856)
XLA Ops:
  0.0 1.5 %maximum_bitcast_fusion = bf16[4,8,176,128]{3,1,2,0:T(8,128)(2,1)S(1)} fusion(bf16[32,2048]{1,0:T(8,128)(2,1)} %param.13, bf16[32,20480]{1,0:T(8,128)(2,1)} %param.12), kind=kLoop, calls=%fused_computation | loop fusion | flops 2883584 | bytes 2883584
  1.5 0.0 copy-start.2
  1.5 0.0 copy-start
  1.5 0.0 copy-start.1
  1.5 0.2 copy.8
  1.7 0.4 copy-done.2
  2.2 0.0 copy-done
  2.2 0.0 copy-done.1
  2.2 81.6 %shard_map.73 = bf16[512,512]{1,0:T(8,128)(2,1)S(1)} custom-call(s32[1,128]{1,0:T(1,128)S(1)} %pad.4.active_ref, s32[1,8]{1,0:T(1,128)S(1)} %copy-done, s32[1,8]{1,0:T(1,128)S(1)} %copy-done.1, bf16[512,5120]{1,0:T(8,128)(2,1)} %tokens_hbm.1, bf16[5120,512]{1,0:T(8,128)(2,1)} %base_hbm.1, bf16[32,176,128]{2,1,0:T(8,128)(2,1)S(1)} %bitcast.3), custom_call_target="tpu_custom_call" | custom-call | tf_op jit(solution)/shard_map/pallas_call | solution.py:222
  83.8 0.8 copy.10
  (1 shorter events, 0.0 us)
Async XLA Ops:
  1.5 0.7 copy-start.2
  1.5 0.7 copy-start
  1.5 0.7 copy-start.1

commit v4 on v1

--- a/solution.py
+++ b/solution.py
@@ -121,8 +121,8 @@
     )
 
     def take_group(t, _):
-        half = (my_half + t) % 2
-        from_group = half * half_groups + (my_group - t // 2 + half_groups) % half_groups
+        half = (my_half + t // half_groups) % 2
+        from_group = half * half_groups + (my_group - t % half_groups + half_groups) % half_groups
 
         def take_core(c, _):
             origin = from_group * group + c

time: 80.3 us -> 80.3 us (level)
  no operation moved by 1% of the time
where the time goes in v4:
time: 80.3 us; the launch traced here: 79.7 us
  Pallas kernels  76.7 us (96%)
  other arithmetic  1.49 us (2%)
  local copies, waits for them, and re-layouts  1.45 us (2%)
    pallas_call x1, Pallas kernels, shards(): pl.pallas_call(functools.partial(kernel, n, down_rows, up_rows), out_shap...  76.7 us

profile of v4, /device:TPU:0, one launch (start us, length us, event | category | flops | bytes accessed | tf_op | source)
XLA Modules:
  0.0 79.7 jit_solution(16341403529641650596)
XLA Ops:
  0.0 1.5 %maximum_bitcast_fusion = bf16[4,8,176,128]{3,1,2,0:T(8,128)(2,1)S(1)} fusion(bf16[32,2048]{1,0:T(8,128)(2,1)} %param.13, bf16[32,20480]{1,0:T(8,128)(2,1)} %param.12), kind=kLoop, calls=%fused_computation | loop fusion | flops 2883584 | bytes 2883584
  1.5 0.0 copy-start.2
  1.5 0.0 copy-start
  1.5 0.0 copy-start.1
  1.5 0.2 copy.8
  1.7 0.4 copy-done.2
  2.2 0.0 copy-done
  2.2 0.0 copy-done.1
  2.2 76.7 %shard_map.73 = bf16[512,512]{1,0:T(8,128)(2,1)S(1)} custom-call(s32[1,128]{1,0:T(1,128)S(1)} %pad.4.active_ref, s32[1,8]{1,0:T(1,128)S(1)} %copy-done, s32[1,8]{1,0:T(1,128)S(1)} %copy-done.1, bf16[512,5120]{1,0:T(8,128)(2,1)} %tokens_hbm.1, bf16[5120,512]{1,0:T(8,128)(2,1)} %base_hbm.1, bf16[32,176,128]{2,1,0:T(8,128)(2,1)S(1)} %bitcast.3), custom_call_target="tpu_custom_call" | custom-call | tf_op jit(solution)/shard_map/pallas_call | solution.py:190
  78.9 0.8 copy.10
  (1 shorter events, 0.0 us)
Async XLA Ops:
  1.5 0.7 copy-start.2
  1.5 0.7 copy-start
  1.5 0.7 copy-start.1
